TPU v7x, 256 devices: a whole 4x4x8 slice. The times are simulated.
256 devices in a mesh: seq: 16 (over y, z_lo, core), row: 4 (over z_hi), col: 4 (over x).
Axes of the slice: x: 4, y: 4, z: 8 (z_hi: 4, z_lo: 2; z = z_hi * 2 + z_lo), core: 2. Of those that a mesh axis runs over, the one named last changes fastest.
Arguments:
- tokens: bfloat16 [8192, 4096], P(('seq', 'row'), 'col'), may hold values from -6 to 6
- w_uvqk: bfloat16 [4096, 8192], P(('seq', 'row'), 'col'), may hold values from -0.09375 to 0.09375
- w_out: bfloat16 [2048, 4096], P('col', ('seq', 'row')), may hold values from -0.375 to 0.375
- rab_table: float32 [16, 32], replicated, may hold values from -4 to 4
- norm_gain: float32 [16, 128], replicated, may hold values from 0.5 to 2
- user_lengths: int32 [4], replicated, may hold values from 1 to 6144, 8192 in all
- bucket_ids: int32 [8192], P('seq'), may hold values from 0 to 8191, as said below
Outputs:
- layer_out: bfloat16 [8192, 4096], P(('seq', 'row'), 'col')
Inputs may be any that keep to these rules, and one draw needn't show every extreme that they name: bucket_ids never fall from one token to the next.
All inputs are finite; a program needn't handle non-finite values.
Results may differ from a plain program's by a relative error of at most 0.014.
Values may be sent and summed in bfloat16 or wider, within the bound.
No kernel may reach another device: no remote copies, remote signals or barrier semaphores. Data moves between devices by JAX's collectives and lax.ppermute only.
A program may use at most 64 MiB of HBM per device.

v0:
```python
import functools

import jax
import jax.numpy as jnp
from jax import lax
from jax.experimental import pallas as pl
from jax.experimental.pallas import tpu as pltpu
from jax.sharding import Mesh
from jax.sharding import PartitionSpec as P

DH = 128
NB = 32
RUN = 128
BLOCK = 512
PAIR = 256
NORM_EPS = 1e-05
SCALE = DH ** (-0.5)


def rotations(value, axis, size, step=1):
    return [value] + [
        lax.ppermute(value, axis, [(i, (i + step * k) % size) for i in range(size)])
        for k in range(1, size)
    ]


def swap(value, axis):
    return lax.ppermute(value, axis, [(0, 1), (1, 0)])


def project_kernel(place, a0, a1, a2, a3, b0, b1, b2, b3, weights, kv_ref, q_ref, u_ref, total):
    y, x = place[0], place[4]
    seconds = (b0, b1, b2, b3)
    for kx, first in enumerate((a0, a1, a2, a3)):
        ky = (y - (x - kx)) & 3
        second = jnp.concatenate([b[kx * RUN : (kx + 1) * RUN, :] for b in seconds], axis=0)
        for m in range(4):
            left = first[...] if m < 2 else second
            right = jnp.concatenate([weights[j * 4 + m, ky, :64, :] for j in range(4)], axis=0)
            part = jnp.dot(
                left[:, (m & 1) * 256 : (m & 1) * 256 + 256], right, preferred_element_type=jnp.float32
            )
            if kx == 0 and m == 0:
                total[...] = part
            else:
                total[...] += part
    half = 0.5 * total[...]
    act = (half + half * jnp.tanh(half)).astype(jnp.bfloat16)
    for r in range(4):
        rows = slice(r * RUN, (r + 1) * RUN)
        u_ref[r] = act[rows, :DH]
        kv_ref[r, :, :DH] = act[rows, DH : 2 * DH]
        q_ref[r] = act[rows, 2 * DH : 3 * DH]
        kv_ref[r, :, DH:] = act[rows, 3 * DH :]


def attend_kernel(
    place,
    lengths,
    q_edges,
    k_edges,
    biases,
    q0,
    q1,
    q2,
    q3,
    kv_near,
    kv_far,
    q_ids,
    k_ids,
    table,
    send_ref,
    queries,
    acc,
):
    y, zl, core, zh = (place[i] for i in range(4))
    block = zl * 2 + core
    end0 = lengths[0]
    end1 = end0 + lengths[1]
    end2 = end1 + lengths[2]

    def user_start(pos):
        return jnp.where(
            pos >= end2, end2, jnp.where(pos >= end1, end1, jnp.where(pos >= end0, end0, 0))
        )

    for kz, source in enumerate((q0, q1, q2, q3)):
        rows = pl.ds(pl.multiple_of(((zh - kz) & 3) * RUN, RUN), RUN)
        for r in range(4):
            queries[r, rows, :] = source[r]
    table_rows = jnp.broadcast_to(table[...], (PAIR, DH))

    @pl.loop(0, 4)
    def _(r):
        group = (y - r) & 3
        first = group * 2048 + block * BLOCK
        start_low, start_high = user_start(first), user_start(first + BLOCK - 1)
        q_low, q_high = q_edges[r, 0], q_edges[r, 1]
        acc[...] = jnp.zeros_like(acc)

        def tile(t, carry):
            ky, zl_from = (y - (t >> 1)) & 3, t & 1
            zx = zl ^ zl_from
            near, far = kv_near[zx, ky], kv_far[zx, ky]
            keys = jnp.concatenate([near[:, DH:], far[:, DH:]], axis=0)
            values = jnp.concatenate([near[:, :DH], far[:, :DH]], axis=0)
            k_first = t * 1024 + zh * RUN
            k_last = k_first + BLOCK + RUN - 1
            gap_low = jnp.clip(q_low - k_edges[ky, zl_from * 2 + 1], 0, NB - 1)
            gap_high = jnp.clip(q_high - k_edges[ky, zl_from * 2], 0, NB - 1)
            plain = (k_last <= first) & (k_first >= start_high) & (gap_low == gap_high)

            def scores(part):
                rows = slice(part * PAIR, (part + 1) * PAIR)
                return rows, lax.dot_general(
                    queries[r, rows, :],
                    keys,
                    (((1,), (1,)), ((), ())),
                    preferred_element_type=jnp.float32,
                ) * (0.5 * SCALE)

            @pl.when(plain)
            def _():
                bias = 0.5 * biases[gap_low]
                for part in range(2):
                    rows, half = scores(part)
                    half = half + bias
                    weights = (half + half * jnp.tanh(half)).astype(jnp.bfloat16)
                    acc[rows, :] += jnp.dot(weights, values, preferred_element_type=jnp.float32)

            @pl.when(jnp.logical_not(plain))
            def _():
                k_row = k_ids[ky, pl.ds(zl_from, 1), :]
                column = lax.broadcasted_iota(jnp.int32, (1, PAIR), 1)
                k_pos = k_first + ((column >> 7) ^ core) * BLOCK + (column & (RUN - 1))
                for part in range(2):
                    rows, half = scores(part)
                    gaps = jnp.clip(q_ids[r, rows, :] - k_row, 0, NB - 1)
                    bias = jnp.concatenate(
                        [
                            jnp.take_along_axis(
                                table_rows,
                                gaps[:, c * DH : (c + 1) * DH],
                                axis=1,
                                mode="promise_in_bounds",
                            )
                            for c in range(PAIR // DH)
                        ],
                        axis=1,
                    )
                    half = half + 0.5 * bias
                    q_pos = first + part * PAIR + lax.broadcasted_iota(jnp.int32, (PAIR, 1), 0)
                    seen = (k_pos <= q_pos) & (k_pos >= user_start(q_pos))
                    silu = half + half * jnp.tanh(half)
                    weights = jnp.where(seen, silu, 0.0).astype(jnp.bfloat16)
                    acc[rows, :] += jnp.dot(weights, values, preferred_element_type=jnp.float32)

            return carry

        lowest = jnp.maximum((start_low - (BLOCK + RUN - 1) - zh * RUN + 1023) >> 10, 0)
        lax.fori_loop(lowest, group * 2 + zl + 1, tile, 0)
        attended = acc[...]
        centered = attended - jnp.mean(attended, axis=-1, keepdims=True)
        for zh_to in range(4):
            rows = slice(zh_to * RUN, (zh_to + 1) * RUN)
            send_ref[group * 4 + zh_to] = centered[rows, :].astype(jnp.bfloat16)


def finish_kernel(place, parts, u0, u1, u2, u3, gain, weights, own_ref, send_ref, gated):
    y, x = place[0], place[4]
    for k, u in enumerate((u0, u1, u2, u3)):
        head = (y + k) & 3
        attended = parts[head * 4].astype(jnp.float32)
        for part in range(1, 4):
            attended += parts[head * 4 + part].astype(jnp.float32)
        mean = jnp.mean(attended, axis=-1, keepdims=True)
        centered = attended - mean
        var = jnp.mean(centered * centered, axis=-1, keepdims=True)
        normed = centered * lax.rsqrt(var + NORM_EPS) * gain[pl.ds(head, 1), :]
        columns = pl.ds(pl.multiple_of(head * DH, DH), DH)
        gated[:, columns] = (normed * u[...].astype(jnp.float32)).astype(jnp.bfloat16)
    for k in range(4):
        ky = (y - x - k) & 3
        for m in range(4):
            columns = slice(m * 256, (m + 1) * 256)
            right = jnp.concatenate([weights[j * 4 + m, ky] for j in range(4)], axis=0)
            part = lax.dot_general(
                gated[...], right, (((1,), (1,)), ((), ())), preferred_element_type=jnp.float32
            )
            if k == 0:
                own_ref[:, columns] = part
            else:
                send_ref[k - 1, :, columns] = part.astype(jnp.bfloat16)


def add_kernel(tokens, own, p1, p2, p3, out_ref):
    total = tokens[...].astype(jnp.float32) + own[...]
    for part in (p1, p2, p3):
        total += part[...].astype(jnp.float32)
    out_ref[...] = total.astype(jnp.bfloat16)


def call(kernel, shapes, n_smem, n_vmem, scratch, flops, moved, vmem, name):
    return pl.pallas_call(
        kernel,
        out_shape=shapes,
        in_specs=[pl.BlockSpec(memory_space=pltpu.SMEM)] * n_smem
        + [pl.BlockSpec(memory_space=pltpu.VMEM)] * n_vmem,
        out_specs=jax.tree.map(lambda _: pl.BlockSpec(memory_space=pltpu.VMEM), shapes),
        scratch_shapes=scratch,
        compiler_params=pltpu.CompilerParams(vmem_limit_bytes=vmem * 2**20),
        cost_estimate=pl.CostEstimate(flops=flops, bytes_accessed=moved, transcendentals=0),
        name=name,
    )


def on_device(tokens, w_uvqk, w_out, rab_table, norm_gain, user_lengths, bucket_ids):
    bf16, f32 = jnp.bfloat16, jnp.float32
    y, zl, core, zh, x = (lax.axis_index(a) for a in ("y", "zl", "core", "zh", "x"))
    place = jnp.stack([y, zl, core, zh, x]).astype(jnp.int32)
    plane = ("zh", "zl", "core")

    ids = jnp.stack([bucket_ids // 128, bucket_ids % 128]).astype(bf16)
    ids = jnp.concatenate([ids, jnp.zeros((14, BLOCK), bf16)], axis=0)

    def columns(owner):
        part = lax.dynamic_slice_in_dim(w_uvqk, owner * 512, 512, 1)
        return jnp.concatenate([part, ids], axis=0)

    pieces = [columns(y)] + [
        lax.ppermute(columns((y + k) & 3), "y", [(i, (i + k) % 4) for i in range(4)])
        for k in range(1, 4)
    ]
    piece = jnp.stack(pieces)
    weights = lax.all_gather(piece, plane)

    travelling, _ = lax.optimization_barrier((tokens, piece))

    first = rotations(jnp.concatenate([travelling[:, :512], w_out.T], axis=0), "y", 4)
    second = rotations(travelling[:, 512:], "x", 4)
    first, second = lax.optimization_barrier((first, second))
    firsts = rotations(jnp.concatenate([f[:RUN] for f in first], axis=0), "x", 4)
    seconds = rotations(jnp.concatenate(second, axis=0), "y", 4)
    wo_rows = jnp.stack([f[RUN:] for f in first])
    firsts, seconds, wo_rows = lax.optimization_barrier((firsts, seconds, wo_rows))

    kv, q, u = call(
        project_kernel,
        [
            jax.ShapeDtypeStruct((4, RUN, 2 * DH), bf16),
            jax.ShapeDtypeStruct((4, RUN, DH), bf16),
            jax.ShapeDtypeStruct((4, RUN, DH), bf16),
        ],
        1,
        9,
        [pltpu.VMEM((512, 512), f32)],
        2 * 512 * 512 * 4096,
        9 * 2**20,
        24,
        "project",
    )(place, *firsts, *seconds, weights)

    wo_rows, _ = lax.optimization_barrier((wo_rows, weights))
    wo_all = lax.all_gather(wo_rows, plane)

    from_zl = swap(kv, "zl")
    later, from_zl = lax.optimization_barrier((q, from_zl))
    kv_near = jnp.stack([kv, from_zl])
    kv_far = swap(kv_near, "core")
    q_all = [q] + [
        lax.ppermute(q if k == 1 else later, "zh", [(i, (i + k) % 4) for i in range(4)])
        for k in range(1, 4)
    ]

    coded = weights[:4, :, 64:66].astype(f32)
    all_ids = (coded[:, :, 0] * 128 + coded[:, :, 1]).astype(jnp.int32).transpose(1, 0, 2)
    q_ids = lax.dynamic_slice(all_ids, (0, zl * 2 + core, 0), (4, 1, BLOCK)).reshape(4, BLOCK, 1)
    q_edges = jnp.concatenate([q_ids[:, 0], q_ids[:, -1]], axis=1)
    k_ids = lax.dynamic_slice(all_ids, (0, 0, zh * RUN), (4, 4, RUN))
    k_edges = jnp.stack([k_ids[:, ::2, 0], k_ids[:, 1::2, -1]], axis=-1).reshape(4, 4)
    k_ids = k_ids.reshape(4, 2, 2, RUN)
    k_ids = jnp.where(core == 0, k_ids, k_ids[:, :, ::-1]).reshape(4, 2, PAIR)
    biases = lax.dynamic_slice(rab_table, (x * 4 + y, 0), (1, NB))
    gains = lax.dynamic_slice(norm_gain, (x * 4, 0), (4, DH))
    table = jnp.pad(biases, ((0, 0), (0, DH - NB)))

    parts = call(
        attend_kernel,
        jax.ShapeDtypeStruct((16, RUN, DH), bf16),
        5,
        9,
        [pltpu.VMEM((4, BLOCK, DH), bf16), pltpu.VMEM((BLOCK, DH), f32)],
        4 * 512 * 4096 * DH,
        5 * 2**20,
        14,
        "attend",
    )(place, user_lengths, q_edges, k_edges, biases[0], *q_all, kv_near, kv_far, q_ids, k_ids, table)

    u, _ = lax.optimization_barrier((u, (kv_far, q_all)))
    u_own = [u[0]] + [
        lax.ppermute(u[k], "y", [(i, (i - k) % 4) for i in range(4)]) for k in range(1, 4)
    ]
    arrived = lax.all_to_all(parts, ("y", "zh"), 0, 0, tiled=True)
    arrived, wo_all = lax.optimization_barrier((arrived, wo_all))
    own, shares = call(
        finish_kernel,
        [jax.ShapeDtypeStruct((RUN, 1024), f32), jax.ShapeDtypeStruct((3, RUN, 1024), bf16)],
        1,
        7,
        [pltpu.VMEM((RUN, 4 * DH), bf16)],
        2 * RUN * 512 * 4096,
        5 * 2**20,
        14,
        "finish",
    )(place, arrived, *u_own, gains, wo_all)
    shares = [
        lax.ppermute(shares[k - 1], "x", [(i, (i + k) % 4) for i in range(4)]) for k in range(1, 4)
    ]
    return call(
        add_kernel,
        jax.ShapeDtypeStruct((RUN, 1024), bf16),
        0,
        5,
        [],
        5 * RUN * 1024,
        2**20,
        8,
        "add",
    )(tokens, own, *shares)


def solution(mesh):
    fine = Mesh(mesh.devices.reshape(4, 2, 2, 4, 4), ("y", "zl", "core", "zh", "x"))
    every = ("y", "zl", "core", "zh")
    placed = (
        P(every, "x"),
        P(every, "x"),
        P("x", every),
        P(),
        P(),
        P(),
        P(("y", "zl", "core")),
    )
    return jax.shard_map(
        on_device, mesh=fine, in_specs=placed, out_specs=P(every, "x"), check_vma=False
    )
```

profile of v0, /device:TPU:32, one launch (start us, length us, event | category | flops | bytes accessed | tf_op | source)
XLA Modules:
  0.0 174.0 jit_solution(200752077754265049)
XLA Ops:
  8.4 1.7 collective-permute-start
  10.1 2.9 %collective-permute-start.1 = (bf16[80,512]{1,0:T(8,128)(2,1)S(1)}, bf16[80,512]{1,0:T(8,128)(2,1)S(1)}, u32[]{:S(2)}, u32[]{:S(2)}) collective-permute-start(bf16[80,512]{1,0:T(8,128)(2,1)S(1)} %get-tuple-element.82), channel_id=1, source_target_pairs={{0,128},{64,192},{128,0},{192,64},{1,129},{65,193},{129,1},{193,65... | collective-permute-start | bytes 245768 | tf_op jit(solution)/shard_map/ppermute | solution.py:231
  14.3 2.6 %collective-permute-done.1 = bf16[80,512]{1,0:T(8,128)(2,1)S(1)} collective-permute-done((bf16[80,512]{1,0:T(8,128)(2,1)S(1)}, bf16[80,512]{1,0:T(8,128)(2,1)S(1)}, u32[]{:S(2)}, u32[]{:S(2)}) %collective-permute-start.1) | collective-permute-done | bytes 81952 | tf_op jit(solution)/shard_map/ppermute | solution.py:231
  19.3 1.6 collective-permute-start.6
  22.5 3.3 %collective-permute-start.4 = (bf16[192,512]{1,0:T(8,128)(2,1)S(1)}, bf16[192,512]{1,0:T(8,128)(2,1)S(1)}, u32[]{:S(2)}, u32[]{:S(2)}) collective-permute-start(bf16[192,512]{1,0:T(8,128)(2,1)S(1)} %pad_maximum_fusion.4), channel_id=1, source_target_pairs={{0,128},{64,192},{128,0},{192,64},{1,129},{65,193},{129,1},{193,65... | collective-permute-start | bytes 589832 | tf_op jit(solution)/shard_map/ppermute | solution.py:22
  26.4 2.7 %collective-permute-start.7 = (bf16[128,512]{1,0:T(8,128)(2,1)S(1)}, bf16[128,512]{1,0:T(8,128)(2,1)S(1)}, u32[]{:S(2)}, u32[]{:S(2)}) collective-permute-start(bf16[128,512]{1,0:T(8,128)(2,1)S(1)} %get-tuple-element.39), channel_id=1, source_target_pairs={{0,2},{1,3},{2,0},{3,1},{4,6},{5,7},{6,4},{7,5},{8,10},{9,11},{10,... | collective-permute-start | bytes 393224 | tf_op jit(solution)/shard_map/ppermute | solution.py:22
  29.1 1.4 collective-permute-start.8
  30.6 2.3 %collective-permute-done.7 = bf16[128,512]{1,0:T(8,128)(2,1)S(1)} collective-permute-done((bf16[128,512]{1,0:T(8,128)(2,1)S(1)}, bf16[128,512]{1,0:T(8,128)(2,1)S(1)}, u32[]{:S(2)}, u32[]{:S(2)}) %collective-permute-start.7) | collective-permute-done | bytes 131104 | tf_op jit(solution)/shard_map/ppermute | solution.py:22
  34.2 1.5 collective-permute-start.12
  35.7 1.5 collective-permute-start.13
  38.6 2.4 %collective-permute-start.10 = (bf16[512,512]{1,0:T(8,128)(2,1)S(1)}, bf16[512,512]{1,0:T(8,128)(2,1)S(1)}, u32[]{:S(2)}, u32[]{:S(2)}) collective-permute-start(bf16[512,512]{1,0:T(8,128)(2,1)S(1)} %pad_maximum_fusion.a0), channel_id=1, source_target_pairs={{0,2},{1,3},{2,0},{3,1},{4,6},{5,7},{6,4},{7,5},{8,10},{9,11},{10,... | collective-permute-start | bytes 1572872 | tf_op jit(solution)/shard_map/ppermute | solution.py:22
  41.0 1.6 collective-permute-start.11
  42.6 5.5 %collective-permute-done.12.b1 = bf16[512,512]{1,0:T(8,128)(2,1)S(1)} collective-permute-done((bf16[512,512]{1,0:T(8,128)(2,1)S(1)}, bf16[512,512]{1,0:T(8,128)(2,1)S(1)}, u32[]{:S(2)}, u32[]{:S(2)}) %collective-permute-start.12) | collective-permute-done | bytes 524320 | tf_op jit(solution)/shard_map/ppermute | solution.py:22
  50.1 8.7 %collective-permute-done.13.b2 = bf16[512,512]{1,0:T(8,128)(2,1)S(1)} collective-permute-done((bf16[512,512]{1,0:T(8,128)(2,1)S(1)}, bf16[512,512]{1,0:T(8,128)(2,1)S(1)}, u32[]{:S(2)}, u32[]{:S(2)}) %collective-permute-start.13) | collective-permute-done | bytes 524320 | tf_op jit(solution)/shard_map/ppermute | solution.py:22
  58.8 2.4 %collective-permute-done.11.a3 = bf16[512,512]{1,0:T(8,128)(2,1)} collective-permute-done((bf16[512,512]{1,0:T(8,128)(2,1)S(1)}, bf16[512,512]{1,0:T(8,128)(2,1)}, u32[]{:S(2)}, u32[]{:S(2)}) %collective-permute-start.11) | collective-permute-done | bytes 524320 | tf_op jit(solution)/shard_map/ppermute | solution.py:22
  65.1 2.5 %copy-done.1 = bf16[64,80,512]{2,1,0:T(8,128)(2,1)S(1)} copy-done((bf16[64,80,512]{2,1,0:T(8,128)(2,1)S(1)}, bf16[64,80,512]{2,1,0:T(8,128)(2,1)}, u32[]{:S(2)}) %copy-start.1) | copy-done | bytes 5242904
  67.6 3.6 %project.1 = (bf16[4,128,256]{2,1,0:T(8,128)(2,1)S(1)}, bf16[4,128,128]{2,1,0:T(8,128)(2,1)S(1)}, bf16[4,128,128]{2,1,0:T(8,128)(2,1)S(1)}) custom-call(s32[5]{0:T(128)S(1)} %stack.75.place, bf16[512,512]{1,0:T(8,128)(2,1)S(1)} %pad_maximum_fusion.a0, bf16[512,512]{1,0:T(8,128)(2,1)} %collective-permute-done.9.a1, ...), custom_call_target="tpu_custom_call" | custom-call | flops 2147483648 | bytes 9437184 | tf_op jit(solution)/shard_map/project/pallas_call | solution.py:247
  71.9 1.7 collective-permute-start.15
  73.8 13.7 %collective-permute-done.16 = bf16[4,128,256]{2,1,0:T(8,128)(2,1)S(1)} collective-permute-done((bf16[4,128,256]{2,1,0:T(8,128)(2,1)S(1)}, bf16[4,128,256]{2,1,0:T(8,128)(2,1)S(1)}, u32[]{:S(2)}, u32[]{:S(2)}) %collective-permute-start.16) | collective-permute-done | bytes 262176 | tf_op jit(solution)/shard_map/ppermute | solution.py:28
  87.8 4.0 %collective-permute-start.17 = (bf16[4,128,128]{2,1,0:T(8,128)(2,1)S(1)}, bf16[4,128,128]{2,1,0:T(8,128)(2,1)S(1)}, u32[]{:S(2)}, u32[]{:S(2)}) collective-permute-start(bf16[4,128,128]{2,1,0:T(8,128)(2,1)S(1)} %get-tuple-element.53.q0), channel_id=1, source_target_pairs={{0,8},{4,12},{8,0},{12,4},{1,9},{5,13},{9,1},{13,5},{2,10},{6,14},... | collective-permute-start | bytes 393224 | tf_op jit(solution)/shard_map/ppermute | solution.py:271
  91.8 2.3 %collective-permute-start.18 = (bf16[4,128,128]{2,1,0:T(8,128)(2,1)S(1)}, bf16[4,128,128]{2,1,0:T(8,128)(2,1)S(1)}, u32[]{:S(2)}, u32[]{:S(2)}) collective-permute-start(bf16[4,128,128]{2,1,0:T(8,128)(2,1)S(1)} %get-tuple-element.53.q0), channel_id=1, source_target_pairs={{0,12},{4,0},{8,4},{12,8},{1,13},{5,1},{9,5},{13,9},{2,14},{6,2},{... | collective-permute-start | bytes 393224 | tf_op jit(solution)/shard_map/ppermute | solution.py:271
  94.9 11.0 %collective-permute-done.17.q2 = bf16[4,128,128]{2,1,0:T(8,128)(2,1)S(1)} collective-permute-done((bf16[4,128,128]{2,1,0:T(8,128)(2,1)S(1)}, bf16[4,128,128]{2,1,0:T(8,128)(2,1)S(1)}, u32[]{:S(2)}, u32[]{:S(2)}) %collective-permute-start.17) | collective-permute-done | bytes 131104 | tf_op jit(solution)/shard_map/ppermute | solution.py:271
  105.9 5.1 %collective-permute-done.18.q3 = bf16[4,128,128]{2,1,0:T(8,128)(2,1)S(1)} collective-permute-done((bf16[4,128,128]{2,1,0:T(8,128)(2,1)S(1)}, bf16[4,128,128]{2,1,0:T(8,128)(2,1)S(1)}, u32[]{:S(2)}, u32[]{:S(2)}) %collective-permute-start.18) | collective-permute-done | bytes 131104 | tf_op jit(solution)/shard_map/ppermute | solution.py:271
  111.0 11.2 %attend.1 = bf16[16,128,128]{2,1,0:T(8,128)(2,1)} custom-call(s32[5]{0:T(128)S(1)} %stack.75.place, s32[4]{0:T(128)S(1)} %copy-done.4, s32[4,2]{1,0:T(4,128)S(1)} %pad_add_fusion.1.q_edges, s32[4,4]{1,0:T(4,128)S(1)} %copy.25.k_edges, f32[32]{0:T(128)S(1)} %fusion.11.biases, bf16[4,128,128]{2,1,0:T(8,128)(2,1)S(1)} %get-tuple-element.53.q0, ...), custom_call_target="tpu_custom_call" | custom-call | flops 1073741824 | bytes 5242880 | tf_op jit(solution)/shard_map/attend/pallas_call | solution.py:287
  122.2 8.1 %all-to-all-start = ((bf16[16,128,128]{2,1,0:T(8,128)(2,1)}), bf16[16,128,128]{2,1,0:T(8,128)(2,1)S(1)}, u32[]{:S(2)}, u32[]{:S(2)}) async-start(bf16[16,128,128]{2,1,0:T(8,128)(2,1)} %attend.1), calls=%async_computation | async-start | bytes 1048576 | tf_op jit(solution)/shard_map/all_to_all | solution.py:303
  130.3 3.2 %collective-permute-start.20 = (bf16[128,128]{1,0:T(8,128)(2,1)S(1)}, bf16[128,128]{1,0:T(8,128)(2,1)S(1)}, u32[]{:S(2)}, u32[]{:S(2)}) collective-permute-start(bf16[128,128]{1,0:T(8,128)(2,1)S(1)} %get-tuple-element.74), channel_id=1, source_target_pairs={{0,192},{64,0},{128,64},{192,128},{1,193},{65,1},{129,65},{193,129... | collective-permute-start | bytes 98312 | tf_op jit(solution)/shard_map/ppermute | solution.py:301
  135.2 11.8 %all-to-all-done.parts = bf16[16,128,128]{2,1,0:T(8,128)(2,1)S(1)} async-done(((bf16[16,128,128]{2,1,0:T(8,128)(2,1)}), bf16[16,128,128]{2,1,0:T(8,128)(2,1)S(1)}, u32[]{:S(2)}, u32[]{:S(2)}) %all-to-all-start) | async-done | bytes 524320 | tf_op jit(solution)/shard_map/all_to_all | solution.py:303
  147.1 2.2 %copy-done.2 = bf16[64,64,512]{2,1,0:T(8,128)(2,1)S(1)} copy-done((bf16[64,64,512]{2,1,0:T(8,128)(2,1)S(1)}, bf16[64,64,512]{2,1,0:T(8,128)(2,1)}, u32[]{:S(2)}) %copy-start.2) | copy-done | bytes 4194328
  149.2 2.1 %finish.1 = (f32[128,1024]{1,0:T(8,128)S(1)}, bf16[3,128,1024]{2,1,0:T(8,128)(2,1)S(1)}) custom-call(s32[5]{0:T(128)S(1)} %stack.75.place, bf16[16,128,128]{2,1,0:T(8,128)(2,1)S(1)} %all-to-all-done.parts, bf16[128,128]{1,0:T(8,128)(2,1)S(1)} %get-tuple-element.75.u0, bf16[128,128]{1,0:T(8,128)(2,1)S(1)} %collective-permute-done.20.u1, ...), custom_call_target="tpu_custom_call" | custom-call | flops 536870912 | bytes 5242880 | tf_op jit(solution)/shard_map/finish/pallas_call | solution.py:305
  151.5 2.0 %collective-permute-start.23 = (bf16[128,1024]{1,0:T(8,128)(2,1)S(1)}, bf16[128,1024]{1,0:T(8,128)(2,1)S(1)}, u32[]{:S(2)}, u32[]{:S(2)}) collective-permute-start(bf16[128,1024]{1,0:T(8,128)(2,1)S(1)} %get-tuple-element.65), channel_id=1, source_target_pairs={{0,1},{1,2},{2,3},{3,0},{4,5},{5,6},{6,7},{7,4},{8,9},{9,10},{10,1... | collective-permute-start | bytes 786440 | tf_op jit(solution)/shard_map/ppermute | solution.py:317
  154.5 2.3 %collective-permute-start.25 = (bf16[128,1024]{1,0:T(8,128)(2,1)S(1)}, bf16[128,1024]{1,0:T(8,128)(2,1)S(1)}, u32[]{:S(2)}, u32[]{:S(2)}) collective-permute-start(bf16[128,1024]{1,0:T(8,128)(2,1)S(1)} %get-tuple-element.63), channel_id=1, source_target_pairs={{0,3},{1,0},{2,1},{3,2},{4,7},{5,4},{6,5},{7,6},{8,11},{9,8},{10,9... | collective-permute-start | bytes 786440 | tf_op jit(solution)/shard_map/ppermute | solution.py:317
  156.8 8.9 %collective-permute-done.23.p1 = bf16[128,1024]{1,0:T(8,128)(2,1)S(1)} collective-permute-done((bf16[128,1024]{1,0:T(8,128)(2,1)S(1)}, bf16[128,1024]{1,0:T(8,128)(2,1)S(1)}, u32[]{:S(2)}, u32[]{:S(2)}) %collective-permute-start.23) | collective-permute-done | bytes 262176 | tf_op jit(solution)/shard_map/ppermute | solution.py:317
  (88 shorter events, 22.6 us)
Async XLA Ops:
  6.5 128.7 %copy-start = (f32[16,128]{1,0:T(8,128)S(1)}, f32[16,128]{1,0:T(8,128)}, u32[]{:S(2)}) copy-start(f32[16,128]{1,0:T(8,128)} %param.11) | copy-start | bytes 24580
  6.5 57.0 %all-gather.5.cloned.1.call-start = ((), (), s32[]{:S(2)}) async-start(), calls=%async_computation.1 | async-start | bytes 5570560 | tf_op jit(solution)/shard_map/all_gather | solution.py:235
  8.4 5.9 %collective-permute-start = (bf16[80,512]{1,0:T(8,128)(2,1)S(1)}, bf16[80,512]{1,0:T(8,128)(2,1)S(1)}, u32[]{:S(2)}, u32[]{:S(2)}) collective-permute-start(bf16[80,512]{1,0:T(8,128)(2,1)S(1)} %get-tuple-element.81), channel_id=1, source_target_pairs={{0,64},{64,128},{128,192},{192,0},{1,65},{65,129},{129,193},{193,1... | collective-permute-start | bytes 245768 | tf_op jit(solution)/shard_map/ppermute | solution.py:231
  10.1 6.8 %collective-permute-start.1 = (bf16[80,512]{1,0:T(8,128)(2,1)S(1)}, bf16[80,512]{1,0:T(8,128)(2,1)S(1)}, u32[]{:S(2)}, u32[]{:S(2)}) collective-permute-start(bf16[80,512]{1,0:T(8,128)(2,1)S(1)} %get-tuple-element.82), channel_id=1, source_target_pairs={{0,128},{64,192},{128,0},{192,64},{1,129},{65,193},{129,1},{193,65... | collective-permute-start | bytes 245768 | tf_op jit(solution)/shard_map/ppermute | solution.py:231
  13.0 4.4 %collective-permute-start.2 = (bf16[80,512]{1,0:T(8,128)(2,1)S(1)}, bf16[80,512]{1,0:T(8,128)(2,1)S(1)}, u32[]{:S(2)}, u32[]{:S(2)}) collective-permute-start(bf16[80,512]{1,0:T(8,128)(2,1)S(1)} %get-tuple-element.83), channel_id=1, source_target_pairs={{0,192},{64,0},{128,64},{192,128},{1,193},{65,1},{129,65},{193,129... | collective-permute-start | bytes 245768 | tf_op jit(solution)/shard_map/ppermute | solution.py:231
  18.2 128.8 %all-gather.7.cloned.1.call-start = ((), (), s32[]{:S(2)}) async-start(), calls=%async_computation.2 | async-start | bytes 4456448 | tf_op jit(solution)/shard_map/all_gather | solution.py:264
  19.3 9.9 %collective-permute-start.6 = (bf16[128,512]{1,0:T(8,128)(2,1)S(1)}, bf16[128,512]{1,0:T(8,128)(2,1)S(1)}, u32[]{:S(2)}, u32[]{:S(2)}) collective-permute-start(bf16[128,512]{1,0:T(8,128)(2,1)S(1)} %get-tuple-element.39), channel_id=1, source_target_pairs={{0,1},{1,2},{2,3},{3,0},{4,5},{5,6},{6,7},{7,4},{8,9},{9,10},{10,1... | collective-permute-start | bytes 393224 | tf_op jit(solution)/shard_map/ppermute | solution.py:22
  21.7 12.4 %collective-permute-start.3 = (bf16[192,512]{1,0:T(8,128)(2,1)S(1)}, bf16[192,512]{1,0:T(8,128)(2,1)S(1)}, u32[]{:S(2)}, u32[]{:S(2)}) collective-permute-start(bf16[192,512]{1,0:T(8,128)(2,1)S(1)} %pad_maximum_fusion.4), channel_id=1, source_target_pairs={{0,64},{64,128},{128,192},{192,0},{1,65},{65,129},{129,193},{193,1... | collective-permute-start | bytes 589832 | tf_op jit(solution)/shard_map/ppermute | solution.py:22
  22.5 11.6 %collective-permute-start.4 = (bf16[192,512]{1,0:T(8,128)(2,1)S(1)}, bf16[192,512]{1,0:T(8,128)(2,1)S(1)}, u32[]{:S(2)}, u32[]{:S(2)}) collective-permute-start(bf16[192,512]{1,0:T(8,128)(2,1)S(1)} %pad_maximum_fusion.4), channel_id=1, source_target_pairs={{0,128},{64,192},{128,0},{192,64},{1,129},{65,193},{129,1},{193,65... | collective-permute-start | bytes 589832 | tf_op jit(solution)/shard_map/ppermute | solution.py:22
  25.8 8.3 %collective-permute-start.5 = (bf16[192,512]{1,0:T(8,128)(2,1)S(1)}, bf16[192,512]{1,0:T(8,128)(2,1)S(1)}, u32[]{:S(2)}, u32[]{:S(2)}) collective-permute-start(bf16[192,512]{1,0:T(8,128)(2,1)S(1)} %pad_maximum_fusion.4), channel_id=1, source_target_pairs={{0,192},{64,0},{128,64},{192,128},{1,193},{65,1},{129,65},{193,129... | collective-permute-start | bytes 589832 | tf_op jit(solution)/shard_map/ppermute | solution.py:22
  26.4 6.5 %collective-permute-start.7 = (bf16[128,512]{1,0:T(8,128)(2,1)S(1)}, bf16[128,512]{1,0:T(8,128)(2,1)S(1)}, u32[]{:S(2)}, u32[]{:S(2)}) collective-permute-start(bf16[128,512]{1,0:T(8,128)(2,1)S(1)} %get-tuple-element.39), channel_id=1, source_target_pairs={{0,2},{1,3},{2,0},{3,1},{4,6},{5,7},{6,4},{7,5},{8,10},{9,11},{10,... | collective-permute-start | bytes 393224 | tf_op jit(solution)/shard_map/ppermute | solution.py:22
  29.1 5.0 %collective-permute-start.8 = (bf16[128,512]{1,0:T(8,128)(2,1)S(1)}, bf16[128,512]{1,0:T(8,128)(2,1)S(1)}, u32[]{:S(2)}, u32[]{:S(2)}) collective-permute-start(bf16[128,512]{1,0:T(8,128)(2,1)S(1)} %get-tuple-element.39), channel_id=1, source_target_pairs={{0,3},{1,0},{2,1},{3,2},{4,7},{5,4},{6,5},{7,6},{8,11},{9,8},{10,9... | collective-permute-start | bytes 393224 | tf_op jit(solution)/shard_map/ppermute | solution.py:22
  34.2 13.9 %collective-permute-start.12 = (bf16[512,512]{1,0:T(8,128)(2,1)S(1)}, bf16[512,512]{1,0:T(8,128)(2,1)S(1)}, u32[]{:S(2)}, u32[]{:S(2)}) collective-permute-start(bf16[512,512]{1,0:T(8,128)(2,1)S(1)} %constant_dynamic-update-slice_fusion.b0), channel_id=1, source_target_pairs={{0,64},{64,128},{128,192},{192,0},{1,65},{65,129},{129,193},{193,1... | collective-permute-start | bytes 1572872 | tf_op jit(solution)/shard_map/ppermute | solution.py:22
  35.7 23.1 %collective-permute-start.13 = (bf16[512,512]{1,0:T(8,128)(2,1)S(1)}, bf16[512,512]{1,0:T(8,128)(2,1)S(1)}, u32[]{:S(2)}, u32[]{:S(2)}) collective-permute-start(bf16[512,512]{1,0:T(8,128)(2,1)S(1)} %constant_dynamic-update-slice_fusion.b0), channel_id=1, source_target_pairs={{0,128},{64,192},{128,0},{192,64},{1,129},{65,193},{129,1},{193,65... | collective-permute-start | bytes 1572872 | tf_op jit(solution)/shard_map/ppermute | solution.py:22
  37.2 21.7 %collective-permute-start.14 = (bf16[512,512]{1,0:T(8,128)(2,1)S(1)}, bf16[512,512]{1,0:T(8,128)(2,1)S(1)}, u32[]{:S(2)}, u32[]{:S(2)}) collective-permute-start(bf16[512,512]{1,0:T(8,128)(2,1)S(1)} %constant_dynamic-update-slice_fusion.b0), channel_id=1, source_target_pairs={{0,192},{64,0},{128,64},{192,128},{1,193},{65,1},{129,65},{193,129... | collective-permute-start | bytes 1572872 | tf_op jit(solution)/shard_map/ppermute | solution.py:22
  38.6 20.3 %collective-permute-start.10 = (bf16[512,512]{1,0:T(8,128)(2,1)S(1)}, bf16[512,512]{1,0:T(8,128)(2,1)S(1)}, u32[]{:S(2)}, u32[]{:S(2)}) collective-permute-start(bf16[512,512]{1,0:T(8,128)(2,1)S(1)} %pad_maximum_fusion.a0), channel_id=1, source_target_pairs={{0,2},{1,3},{2,0},{3,1},{4,6},{5,7},{6,4},{7,5},{8,10},{9,11},{10,... | collective-permute-start | bytes 1572872 | tf_op jit(solution)/shard_map/ppermute | solution.py:22
  41.0 20.2 %collective-permute-start.11 = (bf16[512,512]{1,0:T(8,128)(2,1)S(1)}, bf16[512,512]{1,0:T(8,128)(2,1)}, u32[]{:S(2)}, u32[]{:S(2)}) collective-permute-start(bf16[512,512]{1,0:T(8,128)(2,1)S(1)} %pad_maximum_fusion.a0), channel_id=1, source_target_pairs={{0,3},{1,0},{2,1},{3,2},{4,7},{5,4},{6,5},{7,6},{8,11},{9,8},{10,9... | collective-permute-start | bytes 1572872 | tf_op jit(solution)/shard_map/ppermute | solution.py:22
  48.1 14.0 %collective-permute-start.9 = (bf16[512,512]{1,0:T(8,128)(2,1)S(1)}, bf16[512,512]{1,0:T(8,128)(2,1)}, u32[]{:S(2)}, u32[]{:S(2)}) collective-permute-start(bf16[512,512]{1,0:T(8,128)(2,1)S(1)} %pad_maximum_fusion.a0), channel_id=1, source_target_pairs={{0,1},{1,2},{2,3},{3,0},{4,5},{5,6},{6,7},{7,4},{8,9},{9,10},{10,1... | collective-permute-start | bytes 1572872 | tf_op jit(solution)/shard_map/ppermute | solution.py:22
  67.6 43.4 %copy-start.4 = (s32[4]{0:T(128)S(1)}, s32[4]{0:T(128)}, u32[]{:S(2)}) copy-start(s32[4]{0:T(128)} %lengths.1) | copy-start | bytes 52
  71.2 16.3 %collective-permute-start.16 = (bf16[4,128,256]{2,1,0:T(8,128)(2,1)S(1)}, bf16[4,128,256]{2,1,0:T(8,128)(2,1)S(1)}, u32[]{:S(2)}, u32[]{:S(2)}) collective-permute-start(bf16[4,128,256]{2,1,0:T(8,128)(2,1)S(1)} %get-tuple-element.52), channel_id=1, source_target_pairs={{0,32},{32,0},{1,33},{33,1},{2,34},{34,2},{3,35},{35,3},{4,36},{36... | collective-permute-start | bytes 786440 | tf_op jit(solution)/shard_map/ppermute | solution.py:28
  71.9 23.0 %collective-permute-start.15 = (bf16[4,128,128]{2,1,0:T(8,128)(2,1)S(1)}, bf16[4,128,128]{2,1,0:T(8,128)(2,1)S(1)}, u32[]{:S(2)}, u32[]{:S(2)}) collective-permute-start(bf16[4,128,128]{2,1,0:T(8,128)(2,1)S(1)} %get-tuple-element.53.q0), channel_id=1, source_target_pairs={{0,4},{4,8},{8,12},{12,0},{1,5},{5,9},{9,13},{13,1},{2,6},{6,10},{... | collective-permute-start | bytes 393224 | tf_op jit(solution)/shard_map/ppermute | solution.py:271
  87.6 23.4 %collective-permute-start.19 = (bf16[2,4,128,256]{3,2,1,0:T(8,128)(2,1)S(1)}, bf16[2,4,128,256]{3,2,1,0:T(8,128)(2,1)S(1)}, u32[]{:S(2)}, u32[]{:S(2)}) collective-permute-start(bf16[2,4,128,256]{3,2,1,0:T(8,128)(2,1)S(1)} %pad_maximum_fusion.1.kv_near), channel_id=1, source_target_pairs={{0,16},{16,0},{1,17},{17,1},{2,18},{18,2},{3,19},{19,3},{4,20},{20... | collective-permute-start | bytes 1572872 | tf_op jit(solution)/shard_map/ppermute | solution.py:28
  87.8 18.1 %collective-permute-start.17 = (bf16[4,128,128]{2,1,0:T(8,128)(2,1)S(1)}, bf16[4,128,128]{2,1,0:T(8,128)(2,1)S(1)}, u32[]{:S(2)}, u32[]{:S(2)}) collective-permute-start(bf16[4,128,128]{2,1,0:T(8,128)(2,1)S(1)} %get-tuple-element.53.q0), channel_id=1, source_target_pairs={{0,8},{4,12},{8,0},{12,4},{1,9},{5,13},{9,1},{13,5},{2,10},{6,14},... | collective-permute-start | bytes 393224 | tf_op jit(solution)/shard_map/ppermute | solution.py:271
  91.8 19.2 %collective-permute-start.18 = (bf16[4,128,128]{2,1,0:T(8,128)(2,1)S(1)}, bf16[4,128,128]{2,1,0:T(8,128)(2,1)S(1)}, u32[]{:S(2)}, u32[]{:S(2)}) collective-permute-start(bf16[4,128,128]{2,1,0:T(8,128)(2,1)S(1)} %get-tuple-element.53.q0), channel_id=1, source_target_pairs={{0,12},{4,0},{8,4},{12,8},{1,13},{5,1},{9,5},{13,9},{2,14},{6,2},{... | collective-permute-start | bytes 393224 | tf_op jit(solution)/shard_map/ppermute | solution.py:271
  94.9 71.4 %copy-start.3 = (bf16[128,1024]{1,0:T(8,128)(2,1)S(1)}, bf16[128,1024]{1,0:T(8,128)(2,1)}, u32[]{:S(2)}) copy-start(bf16[128,1024]{1,0:T(8,128)(2,1)} %tokens.1) | copy-start | bytes 786436
  122.2 24.9 %all-to-all-start = ((bf16[16,128,128]{2,1,0:T(8,128)(2,1)}), bf16[16,128,128]{2,1,0:T(8,128)(2,1)S(1)}, u32[]{:S(2)}, u32[]{:S(2)}) async-start(bf16[16,128,128]{2,1,0:T(8,128)(2,1)} %attend.1), calls=%async_computation | async-start | bytes 1048576 | tf_op jit(solution)/shard_map/all_to_all | solution.py:303
  130.3 16.8 %collective-permute-start.20 = (bf16[128,128]{1,0:T(8,128)(2,1)S(1)}, bf16[128,128]{1,0:T(8,128)(2,1)S(1)}, u32[]{:S(2)}, u32[]{:S(2)}) collective-permute-start(bf16[128,128]{1,0:T(8,128)(2,1)S(1)} %get-tuple-element.74), channel_id=1, source_target_pairs={{0,192},{64,0},{128,64},{192,128},{1,193},{65,1},{129,65},{193,129... | collective-permute-start | bytes 98312 | tf_op jit(solution)/shard_map/ppermute | solution.py:301
  133.5 13.6 %collective-permute-start.21 = (bf16[128,128]{1,0:T(8,128)(2,1)S(1)}, bf16[128,128]{1,0:T(8,128)(2,1)S(1)}, u32[]{:S(2)}, u32[]{:S(2)}) collective-permute-start(bf16[128,128]{1,0:T(8,128)(2,1)S(1)} %get-tuple-element.73), channel_id=1, source_target_pairs={{0,128},{64,192},{128,0},{192,64},{1,129},{65,193},{129,1},{193,65... | collective-permute-start | bytes 98312 | tf_op jit(solution)/shard_map/ppermute | solution.py:301
  134.3 12.7 %collective-permute-start.22 = (bf16[128,128]{1,0:T(8,128)(2,1)S(1)}, bf16[128,128]{1,0:T(8,128)(2,1)S(1)}, u32[]{:S(2)}, u32[]{:S(2)}) collective-permute-start(bf16[128,128]{1,0:T(8,128)(2,1)S(1)} %get-tuple-element.72), channel_id=1, source_target_pairs={{0,64},{64,128},{128,192},{192,0},{1,65},{65,129},{129,193},{193,1... | collective-permute-start | bytes 98312 | tf_op jit(solution)/shard_map/ppermute | solution.py:301
  151.5 14.2 %collective-permute-start.23 = (bf16[128,1024]{1,0:T(8,128)(2,1)S(1)}, bf16[128,1024]{1,0:T(8,128)(2,1)S(1)}, u32[]{:S(2)}, u32[]{:S(2)}) collective-permute-start(bf16[128,1024]{1,0:T(8,128)(2,1)S(1)} %get-tuple-element.65), channel_id=1, source_target_pairs={{0,1},{1,2},{2,3},{3,0},{4,5},{5,6},{6,7},{7,4},{8,9},{9,10},{10,1... | collective-permute-start | bytes 786440 | tf_op jit(solution)/shard_map/ppermute | solution.py:317
  153.4 12.3 %collective-permute-start.24 = (bf16[128,1024]{1,0:T(8,128)(2,1)S(1)}, bf16[128,1024]{1,0:T(8,128)(2,1)S(1)}, u32[]{:S(2)}, u32[]{:S(2)}) collective-permute-start(bf16[128,1024]{1,0:T(8,128)(2,1)S(1)} %get-tuple-element.64), channel_id=1, source_target_pairs={{0,2},{1,3},{2,0},{3,1},{4,6},{5,7},{6,4},{7,5},{8,10},{9,11},{10,... | collective-permute-start | bytes 786440 | tf_op jit(solution)/shard_map/ppermute | solution.py:317
  154.5 11.8 %collective-permute-start.25 = (bf16[128,1024]{1,0:T(8,128)(2,1)S(1)}, bf16[128,1024]{1,0:T(8,128)(2,1)S(1)}, u32[]{:S(2)}, u32[]{:S(2)}) collective-permute-start(bf16[128,1024]{1,0:T(8,128)(2,1)S(1)} %get-tuple-element.63), channel_id=1, source_target_pairs={{0,3},{1,0},{2,1},{3,2},{4,7},{5,4},{6,5},{7,6},{8,11},{9,8},{10,9... | collective-permute-start | bytes 786440 | tf_op jit(solution)/shard_map/ppermute | solution.py:317
  (2 other events, 4.7 us)
Sparse Core Ops, SparseCore 0:
  18.3 45.1 all-gather.4
  65.4 53.3 all-gather.6
where the time goes:
time: 174 us
  waiting for transfers between devices  76.6 us (44%)
  starting transfers between devices  53.2 us (31%)
  Pallas kernels  17.8 us (10%)
  between operations  13.7 us (8%)
  local copies, waits for them, and re-layouts  9.16 us (5%)
  other arithmetic  3.51 us (2%)
    ppermute x12, waiting for transfers between devices, rotations(): lax.ppermute(value, axis, [(i, (i + step * k) % size) for i in range(size)])  21 us
    ppermute x12, starting transfers between devices, rotations(): lax.ppermute(value, axis, [(i, (i + step * k) % size) for i in range(size)])  20 us
    ppermute x3, waiting for transfers between devices, on_device(): lax.ppermute(q if k == 1 else later, 'zh', [(i, (i + k) % 4) for i in ran...  16.1 us
    ppermute x2, waiting for transfers between devices, swap(): return lax.ppermute(value, axis, [(0, 1), (1, 0)])  13.7 us
    all_to_all x1, waiting for transfers between devices, on_device(): arrived = lax.all_to_all(parts, ('y', 'zh'), 0, 0, tiled=True)  11.8 us
    pallas_call x1, Pallas kernels, on_device(): call(attend_kernel, jax.ShapeDtypeStruct((16, RUN, DH), bf16), 5, 9, [plt...  11.2 us
    ppermute x3, waiting for transfers between devices, on_device(): lax.ppermute(shares[k - 1], 'x', [(i, (i + k) % 4) for i in range(4)])  9.48 us
    all_to_all x1, starting transfers between devices, on_device(): arrived = lax.all_to_all(parts, ('y', 'zh'), 0, 0, tiled=True)  8.07 us
  transfers between devices with their start and end apart: 29, of which 15 were waited for; matrix products, arithmetic and copies ran while one was open for 3% of the time, Pallas kernels for 9%

commit v1 on v0

--- a/solution.py
+++ b/solution.py
@@ -28,7 +28,8 @@
     return lax.ppermute(value, axis, [(0, 1), (1, 0)])
 
 
-def project_kernel(place, a0, a1, a2, a3, b0, b1, b2, b3, weights, kv_ref, q_ref, u_ref, total):
+def project_kernel(low, place, a0, a1, a2, a3, b0, b1, b2, b3, weights, *outs):
+    *out_refs, total = outs
     y, x = place[0], place[4]
     seconds = (b0, b1, b2, b3)
     for kx, first in enumerate((a0, a1, a2, a3)):
@@ -36,7 +37,14 @@
         second = jnp.concatenate([b[kx * RUN : (kx + 1) * RUN, :] for b in seconds], axis=0)
         for m in range(4):
             left = first[...] if m < 2 else second
-            right = jnp.concatenate([weights[j * 4 + m, ky, :64, :] for j in range(4)], axis=0)
+            rows = [weights[j * 4 + m, ky, :64, :] for j in range(4)]
+            right = jnp.concatenate(
+                [
+                    jnp.concatenate([r[:, c : c + DH] for r in rows], axis=0)
+                    for c in (low, low + 2 * DH)
+                ],
+                axis=1,
+            )
             part = jnp.dot(
                 left[:, (m & 1) * 256 : (m & 1) * 256 + 256], right, preferred_element_type=jnp.float32
             )
@@ -48,10 +56,11 @@
     act = (half + half * jnp.tanh(half)).astype(jnp.bfloat16)
     for r in range(4):
         rows = slice(r * RUN, (r + 1) * RUN)
-        u_ref[r] = act[rows, :DH]
-        kv_ref[r, :, :DH] = act[rows, DH : 2 * DH]
-        q_ref[r] = act[rows, 2 * DH : 3 * DH]
-        kv_ref[r, :, DH:] = act[rows, 3 * DH :]
+        if len(out_refs) == 1:
+            out_refs[0][r] = act[rows, :]
+        else:
+            out_refs[0][r] = act[rows, :DH]
+            out_refs[1][r] = act[rows, DH:]
 
 
 def attend_kernel(
@@ -244,33 +253,30 @@
     wo_rows = jnp.stack([f[RUN:] for f in first])
     firsts, seconds, wo_rows = lax.optimization_barrier((firsts, seconds, wo_rows))
 
-    kv, q, u = call(
-        project_kernel,
-        [
-            jax.ShapeDtypeStruct((4, RUN, 2 * DH), bf16),
-            jax.ShapeDtypeStruct((4, RUN, DH), bf16),
-            jax.ShapeDtypeStruct((4, RUN, DH), bf16),
-        ],
-        1,
-        9,
-        [pltpu.VMEM((512, 512), f32)],
-        2 * 512 * 512 * 4096,
-        9 * 2**20,
-        24,
-        "project",
-    )(place, *firsts, *seconds, weights)
+    def project(place, low, shapes, name):
+        return call(
+            functools.partial(project_kernel, low),
+            shapes,
+            1,
+            9,
+            [pltpu.VMEM((512, 256), f32)],
+            512 * 512 * 4096,
+            9 * 2**20,
+            20,
+            name,
+        )(place, *firsts, *seconds, weights)
+
+    (kv,) = project(place, DH, [jax.ShapeDtypeStruct((4, RUN, 2 * DH), bf16)], "project_kv")
+    after, kv = lax.optimization_barrier((place, kv))
+    u, q = project(after, 0, [jax.ShapeDtypeStruct((4, RUN, DH), bf16)] * 2, "project_uq")
 
     wo_rows, _ = lax.optimization_barrier((wo_rows, weights))
     wo_all = lax.all_gather(wo_rows, plane)
 
-    from_zl = swap(kv, "zl")
-    later, from_zl = lax.optimization_barrier((q, from_zl))
+    from_zl, q = lax.optimization_barrier((swap(kv, "zl"), q))
     kv_near = jnp.stack([kv, from_zl])
     kv_far = swap(kv_near, "core")
-    q_all = [q] + [
-        lax.ppermute(q if k == 1 else later, "zh", [(i, (i + k) % 4) for i in range(4)])
-        for k in range(1, 4)
-    ]
+    q_all = rotations(q, "zh", 4)
 
     coded = weights[:4, :, 64:66].astype(f32)
     all_ids = (coded[:, :, 0] * 128 + coded[:, :, 1]).astype(jnp.int32).transpose(1, 0, 2)

time: 174 us -> 165 us (0.948)
  waiting for transfers between devices: 76.6 us -> 71.2 us
  starting transfers between devices: 53.2 us -> 49 us
    ppermute x12 -> x15, waiting for transfers between devices: 21 us -> 39 us  [rotations(): lax.ppermute(value, axis, [(i, (i + step * k) % size) for i in range(size)])]
    ppermute x3 -> x0, waiting for transfers between devices: 16.1 us -> none  [on_device(): lax.ppermute(q if k == 1 else later, 'zh', [(i, (i + k) % 4) for i in ran...]
    ppermute x3 -> x0, starting transfers between devices: 8.07 us -> none  [on_device(): lax.ppermute(q if k == 1 else later, 'zh', [(i, (i + k) % 4) for i in ran...]
    ppermute x2, waiting for transfers between devices: 13.7 us -> 8.19 us  [swap(): return lax.ppermute(value, axis, [(0, 1), (1, 0)])]
    ppermute x12 -> x15, starting transfers between devices: 20 us -> 25 us  [rotations(): lax.ppermute(value, axis, [(i, (i + step * k) % size) for i in range(size)])]
    pallas_call x1 -> x2, Pallas kernels: 3.62 us -> 4.96 us  [project(): call(functools.partial(project_kernel, low), shapes, 1, 9, [pltpu.VMEM((5...]
  transfers between devices with their start and end apart: 29 -> 29, of which waited for: 15 -> 16; matrix products, arithmetic and copies ran while one was open for 3% -> 3% of each run, Pallas kernels for 9% -> 9%
where the time goes in v1:
time: 165 us
  waiting for transfers between devices  71.2 us (43%)
  starting transfers between devices  49 us (30%)
  Pallas kernels  18.2 us (11%)
  between operations  13.7 us (8%)
  local copies, waits for them, and re-layouts  9.16 us (6%)
  other arithmetic  3.51 us (2%)
    ppermute x15, waiting for transfers between devices, rotations(): lax.ppermute(value, axis, [(i, (i + step * k) % size) for i in range(size)])  39 us
    ppermute x15, starting transfers between devices, rotations(): lax.ppermute(value, axis, [(i, (i + step * k) % size) for i in range(size)])  25 us
    all_to_all x1, waiting for transfers between devices, on_device(): arrived = lax.all_to_all(parts, ('y', 'zh'), 0, 0, tiled=True)  10.5 us
    pallas_call x1, Pallas kernels, on_device(): call(attend_kernel, jax.ShapeDtypeStruct((16, RUN, DH), bf16), 5, 9, [plt...  10.2 us
    ppermute x3, waiting for transfers between devices, on_device(): lax.ppermute(shares[k - 1], 'x', [(i, (i + k) % 4) for i in range(4)])  8.94 us
    ppermute x2, waiting for transfers between devices, swap(): return lax.ppermute(value, axis, [(0, 1), (1, 0)])  8.19 us
    all_to_all x1, starting transfers between devices, on_device(): arrived = lax.all_to_all(parts, ('y', 'zh'), 0, 0, tiled=True)  6.41 us
    ppermute x3, starting transfers between devices, on_device(): lax.ppermute(columns(y + k & 3), 'y', [(i, (i + k) % 4) for i in range(4)])  5.9 us
  transfers between devices with their start and end apart: 29, of which 16 were waited for; matrix products, arithmetic and copies ran while one was open for 3% of the time, Pallas kernels for 9%

profile of v1, /device:TPU:32, one launch (start us, length us, event | category | flops | bytes accessed | tf_op | source)
XLA Modules:
  0.0 164.7 jit_solution(4523794493605959669)
XLA Ops:
  8.4 1.7 %collective-permute-start = (bf16[80,512]{1,0:T(8,128)(2,1)S(1)}, bf16[80,512]{1,0:T(8,128)(2,1)S(1)}, u32[]{:S(2)}, u32[]{:S(2)}) collective-permute-start(bf16[80,512]{1,0:T(8,128)(2,1)S(1)} %get-tuple-element.83), channel_id=1, source_target_pairs={{0,64},{64,128},{128,192},{192,0},{1,65},{65,129},{129,193},{193,1... | collective-permute-start | bytes 245768 | tf_op jit(solution)/shard_map/ppermute | solution.py:240
  10.1 2.9 %collective-permute-start.1 = (bf16[80,512]{1,0:T(8,128)(2,1)S(1)}, bf16[80,512]{1,0:T(8,128)(2,1)S(1)}, u32[]{:S(2)}, u32[]{:S(2)}) collective-permute-start(bf16[80,512]{1,0:T(8,128)(2,1)S(1)} %get-tuple-element.84), channel_id=1, source_target_pairs={{0,128},{64,192},{128,0},{192,64},{1,129},{65,193},{129,1},{193,65... | collective-permute-start | bytes 245768 | tf_op jit(solution)/shard_map/ppermute | solution.py:240
  14.3 2.6 %collective-permute-done.1 = bf16[80,512]{1,0:T(8,128)(2,1)S(1)} collective-permute-done((bf16[80,512]{1,0:T(8,128)(2,1)S(1)}, bf16[80,512]{1,0:T(8,128)(2,1)S(1)}, u32[]{:S(2)}, u32[]{:S(2)}) %collective-permute-start.1) | collective-permute-done | bytes 81952 | tf_op jit(solution)/shard_map/ppermute | solution.py:240
  19.3 1.6 collective-permute-start.6
  22.5 3.3 %collective-permute-start.4 = (bf16[192,512]{1,0:T(8,128)(2,1)S(1)}, bf16[192,512]{1,0:T(8,128)(2,1)S(1)}, u32[]{:S(2)}, u32[]{:S(2)}) collective-permute-start(bf16[192,512]{1,0:T(8,128)(2,1)S(1)} %pad_maximum_fusion.4), channel_id=1, source_target_pairs={{0,128},{64,192},{128,0},{192,64},{1,129},{65,193},{129,1},{193,65... | collective-permute-start | bytes 589832 | tf_op jit(solution)/shard_map/ppermute | solution.py:22
  26.4 2.7 %collective-permute-start.7 = (bf16[128,512]{1,0:T(8,128)(2,1)S(1)}, bf16[128,512]{1,0:T(8,128)(2,1)S(1)}, u32[]{:S(2)}, u32[]{:S(2)}) collective-permute-start(bf16[128,512]{1,0:T(8,128)(2,1)S(1)} %get-tuple-element.40), channel_id=1, source_target_pairs={{0,2},{1,3},{2,0},{3,1},{4,6},{5,7},{6,4},{7,5},{8,10},{9,11},{10,... | collective-permute-start | bytes 393224 | tf_op jit(solution)/shard_map/ppermute | solution.py:22
  30.6 2.3 %collective-permute-done.7 = bf16[128,512]{1,0:T(8,128)(2,1)S(1)} collective-permute-done((bf16[128,512]{1,0:T(8,128)(2,1)S(1)}, bf16[128,512]{1,0:T(8,128)(2,1)S(1)}, u32[]{:S(2)}, u32[]{:S(2)}) %collective-permute-start.7) | collective-permute-done | bytes 131104 | tf_op jit(solution)/shard_map/ppermute | solution.py:22
  34.2 1.5 collective-permute-start.12
  38.6 2.4 %collective-permute-start.10 = (bf16[512,512]{1,0:T(8,128)(2,1)S(1)}, bf16[512,512]{1,0:T(8,128)(2,1)S(1)}, u32[]{:S(2)}, u32[]{:S(2)}) collective-permute-start(bf16[512,512]{1,0:T(8,128)(2,1)S(1)} %pad_maximum_fusion.a0), channel_id=1, source_target_pairs={{0,2},{1,3},{2,0},{3,1},{4,6},{5,7},{6,4},{7,5},{8,10},{9,11},{10,... | collective-permute-start | bytes 1572872 | tf_op jit(solution)/shard_map/ppermute | solution.py:22
  41.0 1.6 collective-permute-start.11
  42.6 5.5 %collective-permute-done.12.b1 = bf16[512,512]{1,0:T(8,128)(2,1)S(1)} collective-permute-done((bf16[512,512]{1,0:T(8,128)(2,1)S(1)}, bf16[512,512]{1,0:T(8,128)(2,1)S(1)}, u32[]{:S(2)}, u32[]{:S(2)}) %collective-permute-start.12) | collective-permute-done | bytes 524320 | tf_op jit(solution)/shard_map/ppermute | solution.py:22
  50.1 8.7 %collective-permute-done.13.b2 = bf16[512,512]{1,0:T(8,128)(2,1)S(1)} collective-permute-done((bf16[512,512]{1,0:T(8,128)(2,1)S(1)}, bf16[512,512]{1,0:T(8,128)(2,1)S(1)}, u32[]{:S(2)}, u32[]{:S(2)}) %collective-permute-start.13) | collective-permute-done | bytes 524320 | tf_op jit(solution)/shard_map/ppermute | solution.py:22
  58.8 2.4 %collective-permute-done.11.a3 = bf16[512,512]{1,0:T(8,128)(2,1)} collective-permute-done((bf16[512,512]{1,0:T(8,128)(2,1)S(1)}, bf16[512,512]{1,0:T(8,128)(2,1)}, u32[]{:S(2)}, u32[]{:S(2)}) %collective-permute-start.11) | collective-permute-done | bytes 524320 | tf_op jit(solution)/shard_map/ppermute | solution.py:22
  65.1 2.5 %copy-done.1 = bf16[64,80,512]{2,1,0:T(8,128)(2,1)S(1)} copy-done((bf16[64,80,512]{2,1,0:T(8,128)(2,1)S(1)}, bf16[64,80,512]{2,1,0:T(8,128)(2,1)}, u32[]{:S(2)}) %copy-start.1) | copy-done | bytes 5242904
  67.6 2.5 %project_kv.1 = bf16[4,128,256]{2,1,0:T(8,128)(2,1)S(1)} custom-call(s32[5]{0:T(128)S(1)} %stack.75.place, bf16[512,512]{1,0:T(8,128)(2,1)S(1)} %pad_maximum_fusion.a0, bf16[512,512]{1,0:T(8,128)(2,1)} %collective-permute-done.9.a1, bf16[512,512]{1,0:T(8,128)(2,1)S(1)} %collective-permute-done.10.a2, bf16[512,512]{1,0:T(8,128)(2,1)} %collective-permute-done.11.a3, ...), custom_call_target="tpu_custom_call" | custom-call | flops 1073741824 | bytes 9437184 | tf_op jit(solution)/shard_map/project_kv/pallas_call | solution.py:257
  71.1 2.5 %project_uq.1 = (bf16[4,128,128]{2,1,0:T(8,128)(2,1)S(1)}, bf16[4,128,128]{2,1,0:T(8,128)(2,1)S(1)}) custom-call(s32[5]{0:T(128)S(1)} %stack.75.place, bf16[512,512]{1,0:T(8,128)(2,1)S(1)} %pad_maximum_fusion.a0, bf16[512,512]{1,0:T(8,128)(2,1)} %collective-permute-done.9.a1, bf16[512,512]{1,0:T(8,128)(2,1)S(1)} %collective-permute-done.10.a2, ...), custom_call_target="tpu_custom_call" | custom-call | flops 1073741824 | bytes 9437184 | tf_op jit(solution)/shard_map/project_uq/pallas_call | solution.py:257
  73.6 8.2 %collective-permute-done.15 = bf16[4,128,256]{2,1,0:T(8,128)(2,1)S(1)} collective-permute-done((bf16[4,128,256]{2,1,0:T(8,128)(2,1)S(1)}, bf16[4,128,256]{2,1,0:T(8,128)(2,1)S(1)}, u32[]{:S(2)}, u32[]{:S(2)}) %collective-permute-start.15) | collective-permute-done | bytes 262176 | tf_op jit(solution)/shard_map/ppermute | solution.py:28
  83.4 1.8 %collective-permute-start.17 = (bf16[4,128,128]{2,1,0:T(8,128)(2,1)S(1)}, bf16[4,128,128]{2,1,0:T(8,128)(2,1)S(1)}, u32[]{:S(2)}, u32[]{:S(2)}) collective-permute-start(bf16[4,128,128]{2,1,0:T(8,128)(2,1)S(1)} %get-tuple-element.55.q0), channel_id=1, source_target_pairs={{0,8},{4,12},{8,0},{12,4},{1,9},{5,13},{9,1},{13,5},{2,10},{6,14},... | collective-permute-start | bytes 393224 | tf_op jit(solution)/shard_map/ppermute | solution.py:22
  85.2 1.9 %collective-permute-start.18 = (bf16[4,128,128]{2,1,0:T(8,128)(2,1)S(1)}, bf16[4,128,128]{2,1,0:T(8,128)(2,1)S(1)}, u32[]{:S(2)}, u32[]{:S(2)}) collective-permute-start(bf16[4,128,128]{2,1,0:T(8,128)(2,1)S(1)} %get-tuple-element.55.q0), channel_id=1, source_target_pairs={{0,12},{4,0},{8,4},{12,8},{1,13},{5,1},{9,5},{13,9},{2,14},{6,2},{... | collective-permute-start | bytes 393224 | tf_op jit(solution)/shard_map/ppermute | solution.py:22
  87.8 8.9 %collective-permute-done.16.q1 = bf16[4,128,128]{2,1,0:T(8,128)(2,1)S(1)} collective-permute-done((bf16[4,128,128]{2,1,0:T(8,128)(2,1)S(1)}, bf16[4,128,128]{2,1,0:T(8,128)(2,1)S(1)}, u32[]{:S(2)}, u32[]{:S(2)}) %collective-permute-start.16) | collective-permute-done | bytes 131104 | tf_op jit(solution)/shard_map/ppermute | solution.py:22
  96.8 4.3 %collective-permute-done.17.q2 = bf16[4,128,128]{2,1,0:T(8,128)(2,1)S(1)} collective-permute-done((bf16[4,128,128]{2,1,0:T(8,128)(2,1)S(1)}, bf16[4,128,128]{2,1,0:T(8,128)(2,1)S(1)}, u32[]{:S(2)}, u32[]{:S(2)}) %collective-permute-start.17) | collective-permute-done | bytes 131104 | tf_op jit(solution)/shard_map/ppermute | solution.py:22
  101.1 4.8 %collective-permute-done.18.q3 = bf16[4,128,128]{2,1,0:T(8,128)(2,1)S(1)} collective-permute-done((bf16[4,128,128]{2,1,0:T(8,128)(2,1)S(1)}, bf16[4,128,128]{2,1,0:T(8,128)(2,1)S(1)}, u32[]{:S(2)}, u32[]{:S(2)}) %collective-permute-start.18) | collective-permute-done | bytes 131104 | tf_op jit(solution)/shard_map/ppermute | solution.py:22
  105.8 10.2 %attend.1 = bf16[16,128,128]{2,1,0:T(8,128)(2,1)} custom-call(s32[5]{0:T(128)S(1)} %stack.75.place, s32[4]{0:T(128)S(1)} %copy-done.4, s32[4,2]{1,0:T(4,128)S(1)} %pad_add_fusion.1.q_edges, s32[4,4]{1,0:T(4,128)S(1)} %copy.25.k_edges, f32[32]{0:T(128)S(1)} %fusion.11.biases, bf16[4,128,128]{2,1,0:T(8,128)(2,1)S(1)} %get-tuple-element.55.q0, ...), custom_call_target="tpu_custom_call" | custom-call | flops 1073741824 | bytes 5242880 | tf_op jit(solution)/shard_map/attend/pallas_call | solution.py:293
  116.1 6.4 %all-to-all-start = ((bf16[16,128,128]{2,1,0:T(8,128)(2,1)}), bf16[16,128,128]{2,1,0:T(8,128)(2,1)S(1)}, u32[]{:S(2)}, u32[]{:S(2)}) async-start(bf16[16,128,128]{2,1,0:T(8,128)(2,1)} %attend.1), calls=%async_computation | async-start | bytes 1048576 | tf_op jit(solution)/shard_map/all_to_all | solution.py:309
  122.5 3.2 %collective-permute-start.20 = (bf16[128,128]{1,0:T(8,128)(2,1)S(1)}, bf16[128,128]{1,0:T(8,128)(2,1)S(1)}, u32[]{:S(2)}, u32[]{:S(2)}) collective-permute-start(bf16[128,128]{1,0:T(8,128)(2,1)S(1)} %get-tuple-element.76), channel_id=1, source_target_pairs={{0,192},{64,0},{128,64},{192,128},{1,193},{65,1},{129,65},{193,129... | collective-permute-start | bytes 98312 | tf_op jit(solution)/shard_map/ppermute | solution.py:307
  127.4 10.5 %all-to-all-done.parts = bf16[16,128,128]{2,1,0:T(8,128)(2,1)S(1)} async-done(((bf16[16,128,128]{2,1,0:T(8,128)(2,1)}), bf16[16,128,128]{2,1,0:T(8,128)(2,1)S(1)}, u32[]{:S(2)}, u32[]{:S(2)}) %all-to-all-start) | async-done | bytes 524320 | tf_op jit(solution)/shard_map/all_to_all | solution.py:309
  138.0 2.2 %copy-done.2 = bf16[64,64,512]{2,1,0:T(8,128)(2,1)S(1)} copy-done((bf16[64,64,512]{2,1,0:T(8,128)(2,1)S(1)}, bf16[64,64,512]{2,1,0:T(8,128)(2,1)}, u32[]{:S(2)}) %copy-start.2) | copy-done | bytes 4194328
  140.2 2.1 %finish.1 = (f32[128,1024]{1,0:T(8,128)S(1)}, bf16[3,128,1024]{2,1,0:T(8,128)(2,1)S(1)}) custom-call(s32[5]{0:T(128)S(1)} %stack.75.place, bf16[16,128,128]{2,1,0:T(8,128)(2,1)S(1)} %all-to-all-done.parts, bf16[128,128]{1,0:T(8,128)(2,1)S(1)} %get-tuple-element.77.u0, bf16[128,128]{1,0:T(8,128)(2,1)S(1)} %collective-permute-done.20.u1, ...), custom_call_target="tpu_custom_call" | custom-call | flops 536870912 | bytes 5242880 | tf_op jit(solution)/shard_map/finish/pallas_call | solution.py:311
  142.4 1.6 collective-permute-start.23
  143.9 3.0 %collective-permute-start.24 = (bf16[128,1024]{1,0:T(8,128)(2,1)S(1)}, bf16[128,1024]{1,0:T(8,128)(2,1)S(1)}, u32[]{:S(2)}, u32[]{:S(2)}) collective-permute-start(bf16[128,1024]{1,0:T(8,128)(2,1)S(1)} %get-tuple-element.66), channel_id=1, source_target_pairs={{0,2},{1,3},{2,0},{3,1},{4,6},{5,7},{6,4},{7,5},{8,10},{9,11},{10,... | collective-permute-start | bytes 786440 | tf_op jit(solution)/shard_map/ppermute | solution.py:323
  148.1 4.0 %collective-permute-done.23.p1 = bf16[128,1024]{1,0:T(8,128)(2,1)S(1)} collective-permute-done((bf16[128,1024]{1,0:T(8,128)(2,1)S(1)}, bf16[128,1024]{1,0:T(8,128)(2,1)S(1)}, u32[]{:S(2)}, u32[]{:S(2)}) %collective-permute-start.23) | collective-permute-done | bytes 262176 | tf_op jit(solution)/shard_map/ppermute | solution.py:323
  152.1 4.9 %collective-permute-done.24.p2 = bf16[128,1024]{1,0:T(8,128)(2,1)S(1)} collective-permute-done((bf16[128,1024]{1,0:T(8,128)(2,1)S(1)}, bf16[128,1024]{1,0:T(8,128)(2,1)S(1)}, u32[]{:S(2)}, u32[]{:S(2)}) %collective-permute-start.24) | collective-permute-done | bytes 262176 | tf_op jit(solution)/shard_map/ppermute | solution.py:323
  (89 shorter events, 26.4 us)
Async XLA Ops:
  6.5 120.9 %copy-start = (f32[16,128]{1,0:T(8,128)S(1)}, f32[16,128]{1,0:T(8,128)}, u32[]{:S(2)}) copy-start(f32[16,128]{1,0:T(8,128)} %param.11) | copy-start | bytes 24580
  6.5 57.0 %all-gather.5.cloned.1.call-start = ((), (), s32[]{:S(2)}) async-start(), calls=%async_computation.1 | async-start | bytes 5570560 | tf_op jit(solution)/shard_map/all_gather | solution.py:244
  8.4 5.9 %collective-permute-start = (bf16[80,512]{1,0:T(8,128)(2,1)S(1)}, bf16[80,512]{1,0:T(8,128)(2,1)S(1)}, u32[]{:S(2)}, u32[]{:S(2)}) collective-permute-start(bf16[80,512]{1,0:T(8,128)(2,1)S(1)} %get-tuple-element.83), channel_id=1, source_target_pairs={{0,64},{64,128},{128,192},{192,0},{1,65},{65,129},{129,193},{193,1... | collective-permute-start | bytes 245768 | tf_op jit(solution)/shard_map/ppermute | solution.py:240
  10.1 6.8 %collective-permute-start.1 = (bf16[80,512]{1,0:T(8,128)(2,1)S(1)}, bf16[80,512]{1,0:T(8,128)(2,1)S(1)}, u32[]{:S(2)}, u32[]{:S(2)}) collective-permute-start(bf16[80,512]{1,0:T(8,128)(2,1)S(1)} %get-tuple-element.84), channel_id=1, source_target_pairs={{0,128},{64,192},{128,0},{192,64},{1,129},{65,193},{129,1},{193,65... | collective-permute-start | bytes 245768 | tf_op jit(solution)/shard_map/ppermute | solution.py:240
  13.0 4.4 %collective-permute-start.2 = (bf16[80,512]{1,0:T(8,128)(2,1)S(1)}, bf16[80,512]{1,0:T(8,128)(2,1)S(1)}, u32[]{:S(2)}, u32[]{:S(2)}) collective-permute-start(bf16[80,512]{1,0:T(8,128)(2,1)S(1)} %get-tuple-element.85), channel_id=1, source_target_pairs={{0,192},{64,0},{128,64},{192,128},{1,193},{65,1},{129,65},{193,129... | collective-permute-start | bytes 245768 | tf_op jit(solution)/shard_map/ppermute | solution.py:240
  18.2 119.7 %all-gather.7.cloned.1.call-start = ((), (), s32[]{:S(2)}) async-start(), calls=%async_computation.2 | async-start | bytes 4456448 | tf_op jit(solution)/shard_map/all_gather | solution.py:274
  19.3 9.9 %collective-permute-start.6 = (bf16[128,512]{1,0:T(8,128)(2,1)S(1)}, bf16[128,512]{1,0:T(8,128)(2,1)S(1)}, u32[]{:S(2)}, u32[]{:S(2)}) collective-permute-start(bf16[128,512]{1,0:T(8,128)(2,1)S(1)} %get-tuple-element.40), channel_id=1, source_target_pairs={{0,1},{1,2},{2,3},{3,0},{4,5},{5,6},{6,7},{7,4},{8,9},{9,10},{10,1... | collective-permute-start | bytes 393224 | tf_op jit(solution)/shard_map/ppermute | solution.py:22
  21.7 12.4 %collective-permute-start.3 = (bf16[192,512]{1,0:T(8,128)(2,1)S(1)}, bf16[192,512]{1,0:T(8,128)(2,1)S(1)}, u32[]{:S(2)}, u32[]{:S(2)}) collective-permute-start(bf16[192,512]{1,0:T(8,128)(2,1)S(1)} %pad_maximum_fusion.4), channel_id=1, source_target_pairs={{0,64},{64,128},{128,192},{192,0},{1,65},{65,129},{129,193},{193,1... | collective-permute-start | bytes 589832 | tf_op jit(solution)/shard_map/ppermute | solution.py:22
  22.5 11.6 %collective-permute-start.4 = (bf16[192,512]{1,0:T(8,128)(2,1)S(1)}, bf16[192,512]{1,0:T(8,128)(2,1)S(1)}, u32[]{:S(2)}, u32[]{:S(2)}) collective-permute-start(bf16[192,512]{1,0:T(8,128)(2,1)S(1)} %pad_maximum_fusion.4), channel_id=1, source_target_pairs={{0,128},{64,192},{128,0},{192,64},{1,129},{65,193},{129,1},{193,65... | collective-permute-start | bytes 589832 | tf_op jit(solution)/shard_map/ppermute | solution.py:22
  25.8 8.3 %collective-permute-start.5 = (bf16[192,512]{1,0:T(8,128)(2,1)S(1)}, bf16[192,512]{1,0:T(8,128)(2,1)S(1)}, u32[]{:S(2)}, u32[]{:S(2)}) collective-permute-start(bf16[192,512]{1,0:T(8,128)(2,1)S(1)} %pad_maximum_fusion.4), channel_id=1, source_target_pairs={{0,192},{64,0},{128,64},{192,128},{1,193},{65,1},{129,65},{193,129... | collective-permute-start | bytes 589832 | tf_op jit(solution)/shard_map/ppermute | solution.py:22
  26.4 6.5 %collective-permute-start.7 = (bf16[128,512]{1,0:T(8,128)(2,1)S(1)}, bf16[128,512]{1,0:T(8,128)(2,1)S(1)}, u32[]{:S(2)}, u32[]{:S(2)}) collective-permute-start(bf16[128,512]{1,0:T(8,128)(2,1)S(1)} %get-tuple-element.40), channel_id=1, source_target_pairs={{0,2},{1,3},{2,0},{3,1},{4,6},{5,7},{6,4},{7,5},{8,10},{9,11},{10,... | collective-permute-start | bytes 393224 | tf_op jit(solution)/shard_map/ppermute | solution.py:22
  29.1 5.0 %collective-permute-start.8 = (bf16[128,512]{1,0:T(8,128)(2,1)S(1)}, bf16[128,512]{1,0:T(8,128)(2,1)S(1)}, u32[]{:S(2)}, u32[]{:S(2)}) collective-permute-start(bf16[128,512]{1,0:T(8,128)(2,1)S(1)} %get-tuple-element.40), channel_id=1, source_target_pairs={{0,3},{1,0},{2,1},{3,2},{4,7},{5,4},{6,5},{7,6},{8,11},{9,8},{10,9... | collective-permute-start | bytes 393224 | tf_op jit(solution)/shard_map/ppermute | solution.py:22
  34.2 13.9 %collective-permute-start.12 = (bf16[512,512]{1,0:T(8,128)(2,1)S(1)}, bf16[512,512]{1,0:T(8,128)(2,1)S(1)}, u32[]{:S(2)}, u32[]{:S(2)}) collective-permute-start(bf16[512,512]{1,0:T(8,128)(2,1)S(1)} %constant_dynamic-update-slice_fusion.b0), channel_id=1, source_target_pairs={{0,64},{64,128},{128,192},{192,0},{1,65},{65,129},{129,193},{193,1... | collective-permute-start | bytes 1572872 | tf_op jit(solution)/shard_map/ppermute | solution.py:22
  35.7 23.1 %collective-permute-start.13 = (bf16[512,512]{1,0:T(8,128)(2,1)S(1)}, bf16[512,512]{1,0:T(8,128)(2,1)S(1)}, u32[]{:S(2)}, u32[]{:S(2)}) collective-permute-start(bf16[512,512]{1,0:T(8,128)(2,1)S(1)} %constant_dynamic-update-slice_fusion.b0), channel_id=1, source_target_pairs={{0,128},{64,192},{128,0},{192,64},{1,129},{65,193},{129,1},{193,65... | collective-permute-start | bytes 1572872 | tf_op jit(solution)/shard_map/ppermute | solution.py:22
  37.2 21.7 %collective-permute-start.14 = (bf16[512,512]{1,0:T(8,128)(2,1)S(1)}, bf16[512,512]{1,0:T(8,128)(2,1)S(1)}, u32[]{:S(2)}, u32[]{:S(2)}) collective-permute-start(bf16[512,512]{1,0:T(8,128)(2,1)S(1)} %constant_dynamic-update-slice_fusion.b0), channel_id=1, source_target_pairs={{0,192},{64,0},{128,64},{192,128},{1,193},{65,1},{129,65},{193,129... | collective-permute-start | bytes 1572872 | tf_op jit(solution)/shard_map/ppermute | solution.py:22
  38.6 20.3 %collective-permute-start.10 = (bf16[512,512]{1,0:T(8,128)(2,1)S(1)}, bf16[512,512]{1,0:T(8,128)(2,1)S(1)}, u32[]{:S(2)}, u32[]{:S(2)}) collective-permute-start(bf16[512,512]{1,0:T(8,128)(2,1)S(1)} %pad_maximum_fusion.a0), channel_id=1, source_target_pairs={{0,2},{1,3},{2,0},{3,1},{4,6},{5,7},{6,4},{7,5},{8,10},{9,11},{10,... | collective-permute-start | bytes 1572872 | tf_op jit(solution)/shard_map/ppermute | solution.py:22
  41.0 20.2 %collective-permute-start.11 = (bf16[512,512]{1,0:T(8,128)(2,1)S(1)}, bf16[512,512]{1,0:T(8,128)(2,1)}, u32[]{:S(2)}, u32[]{:S(2)}) collective-permute-start(bf16[512,512]{1,0:T(8,128)(2,1)S(1)} %pad_maximum_fusion.a0), channel_id=1, source_target_pairs={{0,3},{1,0},{2,1},{3,2},{4,7},{5,4},{6,5},{7,6},{8,11},{9,8},{10,9... | collective-permute-start | bytes 1572872 | tf_op jit(solution)/shard_map/ppermute | solution.py:22
  48.1 14.0 %collective-permute-start.9 = (bf16[512,512]{1,0:T(8,128)(2,1)S(1)}, bf16[512,512]{1,0:T(8,128)(2,1)}, u32[]{:S(2)}, u32[]{:S(2)}) collective-permute-start(bf16[512,512]{1,0:T(8,128)(2,1)S(1)} %pad_maximum_fusion.a0), channel_id=1, source_target_pairs={{0,1},{1,2},{2,3},{3,0},{4,5},{5,6},{6,7},{7,4},{8,9},{9,10},{10,1... | collective-permute-start | bytes 1572872 | tf_op jit(solution)/shard_map/ppermute | solution.py:22
  70.0 11.8 %collective-permute-start.15 = (bf16[4,128,256]{2,1,0:T(8,128)(2,1)S(1)}, bf16[4,128,256]{2,1,0:T(8,128)(2,1)S(1)}, u32[]{:S(2)}, u32[]{:S(2)}) collective-permute-start(bf16[4,128,256]{2,1,0:T(8,128)(2,1)S(1)} %project_kv.1), channel_id=1, source_target_pairs={{0,32},{32,0},{1,33},{33,1},{2,34},{34,2},{3,35},{35,3},{4,36},{36... | collective-permute-start | bytes 786440 | tf_op jit(solution)/shard_map/ppermute | solution.py:28
  71.1 34.8 %copy-start.4 = (s32[4]{0:T(128)S(1)}, s32[4]{0:T(128)}, u32[]{:S(2)}) copy-start(s32[4]{0:T(128)} %lengths.1) | copy-start | bytes 52
  81.9 23.9 %collective-permute-start.19 = (bf16[2,4,128,256]{3,2,1,0:T(8,128)(2,1)S(1)}, bf16[2,4,128,256]{3,2,1,0:T(8,128)(2,1)S(1)}, u32[]{:S(2)}, u32[]{:S(2)}) collective-permute-start(bf16[2,4,128,256]{3,2,1,0:T(8,128)(2,1)S(1)} %pad_maximum_fusion.1.kv_near), channel_id=1, source_target_pairs={{0,16},{16,0},{1,17},{17,1},{2,18},{18,2},{3,19},{19,3},{4,20},{20... | collective-permute-start | bytes 1572872 | tf_op jit(solution)/shard_map/ppermute | solution.py:28
  82.1 14.7 %collective-permute-start.16 = (bf16[4,128,128]{2,1,0:T(8,128)(2,1)S(1)}, bf16[4,128,128]{2,1,0:T(8,128)(2,1)S(1)}, u32[]{:S(2)}, u32[]{:S(2)}) collective-permute-start(bf16[4,128,128]{2,1,0:T(8,128)(2,1)S(1)} %get-tuple-element.55.q0), channel_id=1, source_target_pairs={{0,4},{4,8},{8,12},{12,0},{1,5},{5,9},{9,13},{13,1},{2,6},{6,10},{... | collective-permute-start | bytes 393224 | tf_op jit(solution)/shard_map/ppermute | solution.py:22
  83.4 17.6 %collective-permute-start.17 = (bf16[4,128,128]{2,1,0:T(8,128)(2,1)S(1)}, bf16[4,128,128]{2,1,0:T(8,128)(2,1)S(1)}, u32[]{:S(2)}, u32[]{:S(2)}) collective-permute-start(bf16[4,128,128]{2,1,0:T(8,128)(2,1)S(1)} %get-tuple-element.55.q0), channel_id=1, source_target_pairs={{0,8},{4,12},{8,0},{12,4},{1,9},{5,13},{9,1},{13,5},{2,10},{6,14},... | collective-permute-start | bytes 393224 | tf_op jit(solution)/shard_map/ppermute | solution.py:22
  85.2 20.6 %collective-permute-start.18 = (bf16[4,128,128]{2,1,0:T(8,128)(2,1)S(1)}, bf16[4,128,128]{2,1,0:T(8,128)(2,1)S(1)}, u32[]{:S(2)}, u32[]{:S(2)}) collective-permute-start(bf16[4,128,128]{2,1,0:T(8,128)(2,1)S(1)} %get-tuple-element.55.q0), channel_id=1, source_target_pairs={{0,12},{4,0},{8,4},{12,8},{1,13},{5,1},{9,5},{13,9},{2,14},{6,2},{... | collective-permute-start | bytes 393224 | tf_op jit(solution)/shard_map/ppermute | solution.py:22
  87.8 69.2 %copy-start.3 = (bf16[128,1024]{1,0:T(8,128)(2,1)S(1)}, bf16[128,1024]{1,0:T(8,128)(2,1)}, u32[]{:S(2)}) copy-start(bf16[128,1024]{1,0:T(8,128)(2,1)} %tokens.1) | copy-start | bytes 786436
  116.1 21.9 %all-to-all-start = ((bf16[16,128,128]{2,1,0:T(8,128)(2,1)}), bf16[16,128,128]{2,1,0:T(8,128)(2,1)S(1)}, u32[]{:S(2)}, u32[]{:S(2)}) async-start(bf16[16,128,128]{2,1,0:T(8,128)(2,1)} %attend.1), calls=%async_computation | async-start | bytes 1048576 | tf_op jit(solution)/shard_map/all_to_all | solution.py:309
  122.5 15.5 %collective-permute-start.20 = (bf16[128,128]{1,0:T(8,128)(2,1)S(1)}, bf16[128,128]{1,0:T(8,128)(2,1)S(1)}, u32[]{:S(2)}, u32[]{:S(2)}) collective-permute-start(bf16[128,128]{1,0:T(8,128)(2,1)S(1)} %get-tuple-element.76), channel_id=1, source_target_pairs={{0,192},{64,0},{128,64},{192,128},{1,193},{65,1},{129,65},{193,129... | collective-permute-start | bytes 98312 | tf_op jit(solution)/shard_map/ppermute | solution.py:307
  125.7 12.3 %collective-permute-start.21 = (bf16[128,128]{1,0:T(8,128)(2,1)S(1)}, bf16[128,128]{1,0:T(8,128)(2,1)S(1)}, u32[]{:S(2)}, u32[]{:S(2)}) collective-permute-start(bf16[128,128]{1,0:T(8,128)(2,1)S(1)} %get-tuple-element.75), channel_id=1, source_target_pairs={{0,128},{64,192},{128,0},{192,64},{1,129},{65,193},{129,1},{193,65... | collective-permute-start | bytes 98312 | tf_op jit(solution)/shard_map/ppermute | solution.py:307
  126.6 11.4 %collective-permute-start.22 = (bf16[128,128]{1,0:T(8,128)(2,1)S(1)}, bf16[128,128]{1,0:T(8,128)(2,1)S(1)}, u32[]{:S(2)}, u32[]{:S(2)}) collective-permute-start(bf16[128,128]{1,0:T(8,128)(2,1)S(1)} %get-tuple-element.74), channel_id=1, source_target_pairs={{0,64},{64,128},{128,192},{192,0},{1,65},{65,129},{129,193},{193,1... | collective-permute-start | bytes 98312 | tf_op jit(solution)/shard_map/ppermute | solution.py:307
  142.4 9.8 %collective-permute-start.23 = (bf16[128,1024]{1,0:T(8,128)(2,1)S(1)}, bf16[128,1024]{1,0:T(8,128)(2,1)S(1)}, u32[]{:S(2)}, u32[]{:S(2)}) collective-permute-start(bf16[128,1024]{1,0:T(8,128)(2,1)S(1)} %get-tuple-element.67), channel_id=1, source_target_pairs={{0,1},{1,2},{2,3},{3,0},{4,5},{5,6},{6,7},{7,4},{8,9},{9,10},{10,1... | collective-permute-start | bytes 786440 | tf_op jit(solution)/shard_map/ppermute | solution.py:323
  143.9 13.1 %collective-permute-start.24 = (bf16[128,1024]{1,0:T(8,128)(2,1)S(1)}, bf16[128,1024]{1,0:T(8,128)(2,1)S(1)}, u32[]{:S(2)}, u32[]{:S(2)}) collective-permute-start(bf16[128,1024]{1,0:T(8,128)(2,1)S(1)} %get-tuple-element.66), channel_id=1, source_target_pairs={{0,2},{1,3},{2,0},{3,1},{4,6},{5,7},{6,4},{7,5},{8,10},{9,11},{10,... | collective-permute-start | bytes 786440 | tf_op jit(solution)/shard_map/ppermute | solution.py:323
  147.0 10.1 %collective-permute-start.25 = (bf16[128,1024]{1,0:T(8,128)(2,1)S(1)}, bf16[128,1024]{1,0:T(8,128)(2,1)S(1)}, u32[]{:S(2)}, u32[]{:S(2)}) collective-permute-start(bf16[128,1024]{1,0:T(8,128)(2,1)S(1)} %get-tuple-element.65), channel_id=1, source_target_pairs={{0,3},{1,0},{2,1},{3,2},{4,7},{5,4},{6,5},{7,6},{8,11},{9,8},{10,9... | collective-permute-start | bytes 786440 | tf_op jit(solution)/shard_map/ppermute | solution.py:323
  (2 other events, 4.7 us)
Sparse Core Ops, SparseCore 0:
  18.3 45.1 all-gather.4
  65.4 50.9 all-gather.6
